TPU v7x, 32 devices: a whole 2x2x4 slice. The times are simulated.
32 devices in a mesh: groups: 2 (over x), rows: 16 (over z, y, core).
Axes of the slice: x: 2, y: 2, z: 4, core: 2. Of those that a mesh axis runs over, the one named last changes fastest.
Arguments:
- embeddings: bfloat16 [49152, 1024], P(('groups', 'rows')), parts along dimension 0
- block_cluster: int32 [384], P('groups'), parts along dimension 0, may hold values from 0 to 191, as said below
- pair_blocks: int32 [6720, 2], P(('groups', 'rows')), parts along dimension 0, may hold values from 0 to 191, as said below
Outputs:
- best_match: float32 [49152], P(('groups', 'rows')), parts along dimension 0
There are 2 independent parts, one for each index of `groups`. A program takes and returns all parts, laid end to end along the dimension named above; each array names one. Nothing has to cross between parts.
Inputs may be any that keep to these rules, and one draw needn't show every extreme that they name: `block_cluster`: every cluster is a run of consecutive blocks, at most 24 long; different clusters have different ids. `pair_blocks`: slots 210 * i to 210 * i + 209 belong to device i of rows. Each slot (a, b) has block a on that device and a <= b; the slots with a < b name each pair a < b of same-cluster blocks whose a lies on that device exactly once; the other slots have a == b.
All inputs are finite; a program needn't handle non-finite values.
Results may differ from a plain program's by a relative error of at most 0.0011.
Values may be sent and summed in bfloat16 or wider, within the bound.
No kernel may reach another device: no remote copies, remote signals or barrier semaphores. Data moves between devices by JAX's collectives and lax.ppermute only.
A program may use at most 64 MiB of HBM per device.

v0:
```python
import functools

import jax
import jax.numpy as jnp
from jax import lax
from jax.experimental import pallas as pl
from jax.experimental.pallas import tpu as pltpu
from jax.sharding import PartitionSpec as P

BLOCK = 128
NEVER = -3.0
MIB = 1 << 20
FAR_AWAY = 1 << 20
SIZES = (4, 8, 11, 12)
PIECES = ((4,), (6, 2), (6, 3, 2), (6, 4, 2))
LEADING = 6
SMEM = pltpu.SMEM
VMEM = pltpu.VMEM


def plan_kernel(
    chip_blocks, cluster_ref, rows_ref, way_ref, plan_ref, first_ref, last_ref,
    left_part, right_part, from_left, turn, copied,
):
    size = first_ref.shape[0]
    copies = [
        pltpu.make_async_copy(rows_ref.at[pl.ds(start, size), :], ref, copied.at[index])
        for index, (start, ref) in enumerate(((0, first_ref), (rows_ref.shape[0] - size, last_ref)))
    ]
    for copy in copies:
        copy.start()
    here = chip_blocks // 2
    chips = cluster_ref.shape[0] // chip_blocks
    me = lax.axis_index("rows")

    def run_length(start, step, limit):
        count = jnp.int32(0)
        for jump in (16, 8, 4, 2, 1):
            if jump <= limit:
                further = count + jump
                at = jnp.clip(start + step * further, 0, cluster_ref.shape[0] - 1)
                same = (cluster_ref[at] == cluster_ref[start]) & (further <= limit)
                count = jnp.where(same, further, count)
        return count

    def cost(blocks):
        held = jnp.int32(0)
        for size, below in zip(SIZES, (0,) + SIZES):
            held = jnp.where(blocks > below, size, held)
        return jnp.where(blocks > here, FAR_AWAY, held)

    def forward(boundary, carry):
        best_left, best_right, load_right = carry
        edge = (boundary + 1) * chip_blocks
        behind = run_length(edge, -1, chip_blocks - 1)
        ahead = run_length(edge - 1, 1, chip_blocks - 1)
        left_part[boundary] = behind
        right_part[boundary] = ahead
        load_left = cost(ahead)
        by_left = jnp.maximum(best_left, load_left)
        by_right = jnp.maximum(best_right, load_right + load_left)
        from_left[boundary] = jnp.where(by_left <= by_right, 0, 1)
        stays_right = jnp.maximum(best_right, load_right)
        from_left[chips + boundary] = jnp.where(best_left <= stays_right, 0, 1)
        return jnp.minimum(by_left, by_right), jnp.minimum(best_left, stays_right), cost(behind)

    best_left, best_right, load_right = lax.fori_loop(
        0, chips - 1, forward, (jnp.int32(0), jnp.int32(FAR_AWAY), jnp.int32(0))
    )
    last = jnp.where(best_left <= jnp.maximum(best_right, load_right), 0, 1)

    def backward(step, state):
        boundary = chips - 2 - step
        turn[boundary] = state
        return from_left[state * chips + boundary]

    lax.fori_loop(0, chips - 1, backward, last)
    upper = lax.rem(me, 2)
    mine = lax.div(me, 2) - 1 + upper
    inside = (mine >= 0) & (mine < chips - 1)
    mine = jnp.clip(mine, 0, chips - 2)
    behind, ahead, rightwards = left_part[mine], right_part[mine], turn[mine]
    live = inside & (behind > 0) & (ahead > 0)
    receives = live & (rightwards != upper)
    sent = jnp.where(rightwards == 1, behind, ahead)
    paired = jnp.where(rightwards == 1, ahead, behind)
    middle = lax.div(me, 2) * chip_blocks + here
    below = run_length(middle, -1, here)
    above = run_length(middle - 1, 1, here)
    branch = 1 + rightwards * len(SIZES)
    for bound in SIZES[:-1]:
        branch = branch + (sent > bound).astype(jnp.int32)
    way_ref[0] = jnp.where(live, branch, 0)
    plan_ref[0] = (live & (rightwards == upper)).astype(jnp.int32)
    plan_ref[1] = jnp.where(receives, sent, 0)
    plan_ref[2] = jnp.where(receives, jnp.minimum(paired, here), 0)
    plan_ref[3] = jnp.where(receives, jnp.maximum(paired - here, 0), 0)
    plan_ref[4] = upper
    plan_ref[5] = me * here
    plan_ref[6] = jnp.where(upper == 1, above, below)
    plan_ref[7] = jnp.where(upper == 1, below, above)
    for copy in copies:
        copy.wait()


def make_plan(block_cluster, rows, chip_blocks):
    chips = block_cluster.shape[0] // chip_blocks
    return pl.pallas_call(
        functools.partial(plan_kernel, chip_blocks),
        out_shape=tuple(jax.ShapeDtypeStruct((n,), jnp.int32) for n in (1, 8))
        + (VMEM((LEADING * BLOCK, rows.shape[1]), rows.dtype),) * 2,
        in_specs=[pl.BlockSpec(memory_space=SMEM), pl.BlockSpec(memory_space=pl.ANY)],
        out_specs=(pl.BlockSpec(memory_space=SMEM),) * 2 + (pl.BlockSpec(memory_space=VMEM),) * 2,
        scratch_shapes=[
            SMEM((chips,), jnp.int32),
            SMEM((chips,), jnp.int32),
            SMEM((2 * chips,), jnp.int32),
            SMEM((chips,), jnp.int32),
            pltpu.SemaphoreType.DMA((2,)),
        ],
    )(block_cluster, rows)


def unit(rows):
    broadened = rows.astype(jnp.float32)
    total = jnp.sum(broadened * broadened, axis=1, keepdims=True)
    return (broadened * lax.rsqrt(total + 1e-06)).astype(jnp.bfloat16)


def products(left, right):
    return lax.dot_general(
        left, right, (((1,), (1,)), ((), ())), preferred_element_type=jnp.float32
    )


def local_kernel(cluster_ref, plan_ref, rows_ref, other_ref, chip_ref, best_ref):
    blocks = rows_ref.shape[0] // BLOCK
    upper, first, theirs = plan_ref[4], plan_ref[5], plan_ref[7]
    tall, wide = 4, 2
    size = wide * BLOCK

    def normalise(turn, _):
        at = pl.ds(pl.multiple_of(turn * size, size), size)
        chip_ref[at, :] = unit(rows_ref[at, :])
        return 0

    lax.fori_loop(0, blocks // wide, normalise, 0)

    def normalise_other(turn, _):
        start = pl.multiple_of(turn * size, size)
        chip_ref[pl.ds(start + blocks * BLOCK, size), :] = unit(other_ref[pl.ds(start, size), :])
        return 0

    their_from = jnp.where(upper == 1, blocks - theirs, 0)
    their_tiles = lax.div(their_from, wide), lax.div(their_from + theirs + wide - 1, wide)
    lax.fori_loop(their_tiles[0], their_tiles[1], normalise_other, 0)
    best_ref[...] = jnp.full(best_ref.shape, NEVER, jnp.float32)

    def tile(turn, _):
        columns = pl.ds(pl.multiple_of(turn * size, size), size)

        def part(step, _):
            own_part = step < blocks // tall
            other_first = first + blocks - 2 * blocks * upper
            here = jnp.where(own_part, first + step * tall, other_first + step * tall - blocks)
            same = [
                [cluster_ref[here + i] == cluster_ref[first + turn * wide + j] for i in range(tall)]
                for j in range(wide)
            ]
            some = functools.reduce(jnp.logical_or, same[0] + same[1])

            @pl.when(some)
            def _():
                rows = pl.ds(pl.multiple_of(step * tall * BLOCK, tall * BLOCK), tall * BLOCK)
                product = products(chip_ref[rows, :], chip_ref[columns, :])
                row = lax.broadcasted_iota(jnp.int32, product.shape, 0) + step * tall * BLOCK
                column = lax.broadcasted_iota(jnp.int32, product.shape, 1) + turn * size
                product = jnp.where(row == column, NEVER, product)
                for j in range(wide):
                    at = pl.ds(turn * wide + j, 1)
                    best = best_ref[at, :]
                    for i in range(tall):
                        piece = product[i * BLOCK : (i + 1) * BLOCK, j * BLOCK : (j + 1) * BLOCK]
                        top = jnp.max(piece, axis=0, keepdims=True)
                        best = jnp.maximum(best, jnp.where(same[j][i], top, NEVER))
                    best_ref[at, :] = best

            return 0

        lax.fori_loop(0, 2 * blocks // tall, part, 0)
        return 0

    lax.fori_loop(0, blocks // wide, tile, 0)


def local_best(block_cluster, plan, rows, other):
    blocks = rows.shape[0] // BLOCK
    flops = 4 * rows.shape[0] * rows.shape[0] * rows.shape[1]
    vmem = pl.BlockSpec(memory_space=VMEM)
    return pl.pallas_call(
        local_kernel,
        out_shape=(
            VMEM((2 * rows.shape[0], rows.shape[1]), jnp.bfloat16),
            jax.ShapeDtypeStruct((blocks, BLOCK), jnp.float32),
        ),
        in_specs=[pl.BlockSpec(memory_space=SMEM)] * 2 + [vmem] * 2,
        out_specs=(vmem, vmem),
        compiler_params=pltpu.CompilerParams(vmem_limit_bytes=20 * MIB),
        cost_estimate=pl.CostEstimate(flops=flops, bytes_accessed=8 * rows.size, transcendentals=0),
    )(block_cluster, plan, rows, other)


def cross_kernel(start, tall, wide, plan_ref, got_ref, chip_ref, *refs):
    blocks = chip_ref.shape[0] // BLOCK // 2
    half = 16
    rows, row_best, chip_best = refs[-3:]
    back_ref, near_best_ref, far_best_ref = refs[-6:-3]
    count, near, far, upper = plan_ref[1], plan_ref[2], plan_ref[3], plan_ref[4]
    befores = refs[: len(refs) - 6]
    for ref, before in zip((near_best_ref, far_best_ref, back_ref), befores):
        ref[...] = before[...]
    for ref in (near_best_ref, far_best_ref, back_ref)[len(befores) :]:
        ref[...] = jnp.full(ref.shape, NEVER, jnp.float32)
    got_from = jnp.where(upper == 1, 0, blocks - count)
    got_to = got_from + count
    near_from = jnp.where(upper == 1, blocks - near, 0)
    far_from = blocks + jnp.where(upper == 1, blocks - far, 0)
    near_tile, far_tile = lax.div(near_from, wide), lax.div(far_from, wide)
    near_tiles = lax.div(near_from + near + wide - 1, wide) - near_tile
    far_tiles = lax.div(far_from + far + wide - 1, wide) - far_tile

    def part(step, _):
        at = pl.ds(pl.multiple_of(step * tall * BLOCK, tall * BLOCK), tall * BLOCK)
        rows[...] = unit(got_ref[at, :])
        row_best[...] = jnp.full(row_best.shape, NEVER, jnp.float32)
        first = start + step * tall
        fits_in = [(first + i >= got_from) & (first + i < got_to) for i in range(tall)]

        def tile(turn, _):
            turn = jnp.where(turn < near_tiles, near_tile + turn, far_tile + turn - near_tiles)
            side = chip_ref[pl.ds(pl.multiple_of(turn * wide * BLOCK, wide * BLOCK), wide * BLOCK), :]
            product = products(rows[...], side)
            for j in range(wide):
                block = turn * wide + j
                fits = ((block >= near_from) & (block < near_from + near)) | (
                    (block >= far_from) & (block < far_from + far)
                )
                best = jnp.full((1, BLOCK), NEVER, jnp.float32)
                for i in range(tall):
                    at = slice(i * BLOCK, (i + 1) * BLOCK)
                    piece = product[at, j * BLOCK : (j + 1) * BLOCK]
                    row_best[at, :] = jnp.maximum(row_best[at, :], jnp.where(fits, piece, NEVER))
                    top = jnp.max(piece, axis=0, keepdims=True)
                    best = jnp.maximum(best, jnp.where(fits_in[i] & fits, top, NEVER))
                at = pl.ds(jnp.where(block < blocks, block, block - blocks + half), 1)
                chip_best[at, :] = jnp.maximum(chip_best[at, :], best)
            return 0

        lax.fori_loop(0, near_tiles + far_tiles, tile, 0)
        for i in range(tall):
            top = jnp.max(row_best[i * BLOCK : (i + 1) * BLOCK, :].T, axis=0, keepdims=True)
            back_ref[pl.ds(first + i, 1), :] = jnp.where(fits_in[i], top, NEVER)
        return 0

    @pl.when(count > 0)
    def _():
        chip_best[...] = jnp.full(chip_best.shape, NEVER, jnp.float32)
        lax.fori_loop(0, got_ref.shape[0] // BLOCK // tall, part, 0)
        near_best_ref[...] = jnp.maximum(near_best_ref[...], chip_best[0:blocks, :])
        far_best_ref[...] = jnp.maximum(far_best_ref[...], chip_best[half : half + blocks, :])


def cross_best(plan, start, got, chip, before, wide):
    blocks = chip.shape[0] // BLOCK // 2
    features = chip.shape[1]
    pieces = got.shape[0] // BLOCK
    tall = max(tall for tall in (1, 2, 3, 4) if pieces % tall == 0)
    out = jax.ShapeDtypeStruct((blocks, BLOCK), jnp.float32)
    vmem = pl.BlockSpec(memory_space=VMEM)
    flops = 2 * got.shape[0] * blocks * BLOCK * features
    return pl.pallas_call(
        functools.partial(cross_kernel, start, tall, wide),
        out_shape=(out, out, out),
        in_specs=[pl.BlockSpec(memory_space=SMEM)] + [vmem] * (2 + len(before)),
        out_specs=(vmem, vmem, vmem),
        scratch_shapes=[
            VMEM((tall * BLOCK, features), jnp.bfloat16),
            VMEM((tall * BLOCK, BLOCK), jnp.float32),
            VMEM((32, BLOCK), jnp.float32),
        ],
        compiler_params=pltpu.CompilerParams(vmem_limit_bytes=16 * MIB),
        cost_estimate=pl.CostEstimate(flops=flops, bytes_accessed=4 * got.size, transcendentals=0),
    )(plan, got, chip, *before)


def on_device(embeddings, block_cluster, pair_blocks):
    blocks = embeddings.shape[0] // BLOCK
    devices = lax.axis_size("rows")
    swap = [(i, i ^ 1) for i in range(devices)]
    leftwards = [(i + 1, i) for i in range(1, devices - 1, 2)]
    rightwards = [(b, a) for a, b in leftwards]

    other = lax.ppermute(embeddings, "rows", swap)
    way, plan, first, last = make_plan(block_cluster, embeddings, 2 * blocks)

    def send(route, back_route, pieces):
        to_left = route is leftwards

        def branch(embeddings, first, last, other):
            starts = []
            done = 0
            for piece in pieces:
                starts.append(done if to_left else blocks - done - piece)
                done += piece
            got = []
            for start, piece in zip(starts, pieces):
                if piece == LEADING:
                    part = first if to_left else last
                else:
                    part = embeddings[start * BLOCK : (start + piece) * BLOCK]
                got.append(lax.ppermute(part, "rows", route))
            chip, best = local_best(block_cluster, plan, embeddings, other)
            found = (best,)
            for start, piece in zip(starts, got):
                wide = 4 if start == starts[-1] else 2
                back, near, far = cross_best(plan, start, piece, chip, found, wide)
                found = near, far, back
            return near, far, lax.ppermute(back, "rows", back_route)

        return branch

    def stay(embeddings, first, last, other):
        _, best = local_best(block_cluster, plan, embeddings, other)
        nothing = jnp.full((blocks, BLOCK), NEVER, jnp.float32)
        return best, nothing, nothing

    sends = [send(leftwards, rightwards, pieces) for pieces in PIECES]
    sends += [send(rightwards, leftwards, pieces) for pieces in PIECES]
    best, far_best, returned = lax.switch(
        way[0], [stay] + sends, embeddings, first, last, other
    )
    best = jnp.maximum(best, lax.ppermute(far_best, "rows", swap))
    best = jnp.where(plan[0] > 0, jnp.maximum(best, returned), best)
    return best.reshape(-1)


def solution(mesh):
    placed = (P(("groups", "rows"), None), P("groups"), P(("groups", "rows"), None))
    return jax.shard_map(
        on_device, mesh=mesh, in_specs=placed, out_specs=P(("groups", "rows")), check_vma=False
    )
```

profile of v0, /device:TPU:8, one launch (start us, length us, event | category | flops | bytes accessed | tf_op | source)
XLA Modules:
  0.0 51.8 jit_solution(5609952867383615756)
XLA Ops:
  0.0 0.0 copy-start.2
  0.0 0.0 collective-permute-start.26
  0.0 3.3 %shard_map.28 = (s32[1]{0:T(128)}, s32[8]{0:T(128)S(1)}, bf16[768,1024]{1,0:T(8,128)(2,1)S(1)}, bf16[768,1024]{1,0:T(8,128)(2,1)S(1)}) custom-call(s32[192]{0:T(256)} %cluster_ref.1, bf16[1536,1024]{1,0:T(8,128)(2,1)} %rows_ref.1), custom_call_target="tpu_custom_call" | custom-call | tf_op jit(solution)/shard_map/pallas_call | solution.py:108
  4.0 2.0 %collective-permute-done.26 = bf16[1536,1024]{1,0:T(8,128)(2,1)} collective-permute-done((bf16[1536,1024]{1,0:T(8,128)(2,1)}, bf16[1536,1024]{1,0:T(8,128)(2,1)}, u32[]{:S(2)}, u32[]{:S(2)}) %collective-permute-start.26) | collective-permute-done | bytes 3145760 | tf_op jit(solution)/shard_map/ppermute | solution.py:303
  6.0 0.0 copy-done.2
  6.0 43.3 %conditional.1 = (f32[12,128]{1,0:T(8,128)S(1)}, f32[12,128]{1,0:T(8,128)S(1)}, f32[12,128]{1,0:T(8,128)}) conditional(s32[]{:T(128)} %bitcast.1, (s32[192]{0:T(256)S(1)}, s32[8]{0:T(128)S(1)}, bf16[1536,1024]{1,0:T(8,128)(2,1)}, bf16[1536,1024]{1,0:T(8,128)(2,1)}) %tuple.54, (bf16[1536,1024]{1,0:T(8,128)(2,1)}, ...), branch_computations={%region_0.0_spmd, %region_1.0_spmd, %region_2.0_spmd, %region_3.0_... | conditional | flops 14495514624 | bytes 47210708 | solution.py:339
  6.0 3.1 %collective-permute-start.7 = (bf16[768,1024]{1,0:T(8,128)(2,1)S(1)}, bf16[768,1024]{1,0:T(8,128)(2,1)S(1)}, u32[]{:S(2)}, u32[]{:S(2)}) collective-permute-start(bf16[768,1024]{1,0:T(8,128)(2,1)S(1)} %get-tuple-element.121), channel_id=1, source_target_pairs={{2,1},{4,3},{6,5},{8,7},{10,9},{12,11},{14,13},{18,17},{20,19},{22... | collective-permute-start | bytes 4718600 | tf_op jit(solution)/shard_map/cond/branch_3_fun/ppermute | solution.py:321
  9.2 1.2 %slice.29 = bf16[384,1024]{1,0:T(8,128)(2,1)S(1)} slice(bf16[1536,1024]{1,0:T(8,128)(2,1)} %get-tuple-element.117.rows_ref), slice={[768:1152], [0:1024]} | slice | bytes 1572864 | tf_op jit(solution)/shard_map/cond/branch_3_fun/slice | solution.py:320
  10.3 1.3 %collective-permute-start.6 = (bf16[384,1024]{1,0:T(8,128)(2,1)S(1)}, bf16[384,1024]{1,0:T(8,128)(2,1)S(1)}, u32[]{:S(2)}, u32[]{:S(2)}) collective-permute-start(bf16[384,1024]{1,0:T(8,128)(2,1)S(1)} %slice.29), channel_id=1, source_target_pairs={{2,1},{4,3},{6,5},{8,7},{10,9},{12,11},{14,13},{18,17},{20,19},{22... | collective-permute-start | bytes 2359304 | tf_op jit(solution)/shard_map/cond/branch_3_fun/ppermute | solution.py:321
  11.7 1.1 %slice.28 = bf16[256,1024]{1,0:T(8,128)(2,1)S(1)} slice(bf16[1536,1024]{1,0:T(8,128)(2,1)} %get-tuple-element.117.rows_ref), slice={[1152:1408], [0:1024]} | slice | bytes 1048576 | tf_op jit(solution)/shard_map/cond/branch_3_fun/slice | solution.py:320
  12.8 1.3 %collective-permute-start.5 = (bf16[256,1024]{1,0:T(8,128)(2,1)S(1)}, bf16[256,1024]{1,0:T(8,128)(2,1)S(1)}, u32[]{:S(2)}, u32[]{:S(2)}) collective-permute-start(bf16[256,1024]{1,0:T(8,128)(2,1)S(1)} %slice.28), channel_id=1, source_target_pairs={{2,1},{4,3},{6,5},{8,7},{10,9},{12,11},{14,13},{18,17},{20,19},{22... | collective-permute-start | bytes 1572872 | tf_op jit(solution)/shard_map/cond/branch_3_fun/ppermute | solution.py:321
  14.1 15.1 %branch_3_fun.4 = (bf16[3072,1024]{1,0:T(8,128)(2,1)S(1)}, f32[12,128]{1,0:T(8,128)S(1)}) custom-call(s32[192]{0:T(256)S(1)} %get-tuple-element.118.cluster_ref, s32[8]{0:T(128)S(1)} %get-tuple-element.116.plan_ref, bf16[1536,1024]{1,0:T(8,128)(2,1)} %get-tuple-element.117.rows_ref, bf16[1536,1024]{1,0:T(8,128)(2,1)} %get-tuple-element.119.other_ref), custom_call_target="tpu_custom_call" | custom-call | flops 9663676416 | bytes 12582912 | tf_op jit(solution)/shard_map/cond/branch_3_fun/pallas_call | solution.py:200
  29.2 0.0 collective-permute-done.7.got_ref
  29.2 0.6 %branch_3_fun.5 = (f32[12,128]{1,0:T(8,128)S(1)}, f32[12,128]{1,0:T(8,128)S(1)}, f32[12,128]{1,0:T(8,128)S(1)}) custom-call(s32[8]{0:T(128)S(1)} %get-tuple-element.116.plan_ref, bf16[768,1024]{1,0:T(8,128)(2,1)S(1)} %collective-permute-done.7.got_ref, bf16[3072,1024]{1,0:T(8,128)(2,1)S(1)} %get-tuple-element.120.chip_ref, ...), custom_call_target="tpu_custom_call" | custom-call | flops 2415919104 | bytes 3145728 | tf_op jit(solution)/shard_map/cond/branch_3_fun/pallas_call | solution.py:281
  29.8 5.6 %collective-permute-done.6.got_ref = bf16[384,1024]{1,0:T(8,128)(2,1)S(1)} collective-permute-done((bf16[384,1024]{1,0:T(8,128)(2,1)S(1)}, bf16[384,1024]{1,0:T(8,128)(2,1)S(1)}, u32[]{:S(2)}, u32[]{:S(2)}) %collective-permute-start.6) | collective-permute-done | bytes 786464 | tf_op jit(solution)/shard_map/cond/branch_3_fun/ppermute | solution.py:321
  35.4 0.6 %branch_3_fun.6 = (f32[12,128]{1,0:T(8,128)S(1)}, f32[12,128]{1,0:T(8,128)S(1)}, f32[12,128]{1,0:T(8,128)S(1)}) custom-call(s32[8]{0:T(128)S(1)} %get-tuple-element.116.plan_ref, bf16[384,1024]{1,0:T(8,128)(2,1)S(1)} %collective-permute-done.6.got_ref, bf16[3072,1024]{1,0:T(8,128)(2,1)S(1)} %get-tuple-element.120.chip_ref, ...), custom_call_target="tpu_custom_call" | custom-call | flops 1207959552 | bytes 1572864 | tf_op jit(solution)/shard_map/cond/branch_3_fun/pallas_call | solution.py:281
  36.0 5.1 %collective-permute-done.5.got_ref = bf16[256,1024]{1,0:T(8,128)(2,1)S(1)} collective-permute-done((bf16[256,1024]{1,0:T(8,128)(2,1)S(1)}, bf16[256,1024]{1,0:T(8,128)(2,1)S(1)}, u32[]{:S(2)}, u32[]{:S(2)}) %collective-permute-start.5) | collective-permute-done | bytes 524320 | tf_op jit(solution)/shard_map/cond/branch_3_fun/ppermute | solution.py:321
  41.0 0.6 %branch_3_fun.7 = (f32[12,128]{1,0:T(8,128)S(1)}, f32[12,128]{1,0:T(8,128)S(1)}, f32[12,128]{1,0:T(8,128)S(1)}) custom-call(s32[8]{0:T(128)S(1)} %get-tuple-element.116.plan_ref, bf16[256,1024]{1,0:T(8,128)(2,1)S(1)} %collective-permute-done.5.got_ref, bf16[3072,1024]{1,0:T(8,128)(2,1)S(1)} %get-tuple-element.120.chip_ref, ...), custom_call_target="tpu_custom_call" | custom-call | flops 805306368 | bytes 1048576 | tf_op jit(solution)/shard_map/cond/branch_3_fun/pallas_call | solution.py:281
  41.6 1.3 %collective-permute-start.8 = (f32[12,128]{1,0:T(8,128)S(1)}, f32[12,128]{1,0:T(8,128)}, u32[]{:S(2)}, u32[]{:S(2)}) collective-permute-start(f32[12,128]{1,0:T(8,128)S(1)} %get-tuple-element.131), channel_id=1, source_target_pairs={{1,2},{3,4},{5,6},{7,8},{9,10},{11,12},{13,14},{17,18},{19,20},{21... | collective-permute-start | bytes 18440 | tf_op jit(solution)/shard_map/cond/branch_3_fun/ppermute | solution.py:328
  42.9 6.5 %collective-permute-done.8 = f32[12,128]{1,0:T(8,128)} collective-permute-done((f32[12,128]{1,0:T(8,128)S(1)}, f32[12,128]{1,0:T(8,128)}, u32[]{:S(2)}, u32[]{:S(2)}) %collective-permute-start.8) | collective-permute-done | bytes 6176 | tf_op jit(solution)/shard_map/cond/branch_3_fun/ppermute | solution.py:328
  49.3 0.0 collective-permute-start.27
  49.4 1.1 %collective-permute-done.27 = f32[12,128]{1,0:T(8,128)S(1)} collective-permute-done((f32[12,128]{1,0:T(8,128)S(1)}, f32[12,128]{1,0:T(8,128)S(1)}, u32[]{:S(2)}, u32[]{:S(2)}) %collective-permute-start.27) | collective-permute-done | bytes 6176 | tf_op jit(solution)/shard_map/ppermute | solution.py:342
  50.5 1.3 %fusion = f32[1536]{0:T(1024)} fusion(f32[12,128]{1,0:T(8,128)} %get-tuple-element.215, f32[12,128]{1,0:T(8,128)S(1)} %get-tuple-element.213, f32[12,128]{1,0:T(8,128)S(1)} %collective-permute-done.27, pred[]{:T(512)} %bitcast), kind=kLoop, calls=%fused_computation.1 | loop fusion | flops 4608 | bytes 24577 | tf_op jit(solution)/shard_map/reshape | solution.py:344
Async XLA Ops:
  0.0 6.0 %copy-start.2 = (s32[192]{0:T(256)S(1)}, s32[192]{0:T(256)}, u32[]{:S(2)}) copy-start(s32[192]{0:T(256)} %cluster_ref.1) | copy-start | bytes 2308
  0.0 6.0 %collective-permute-start.26 = (bf16[1536,1024]{1,0:T(8,128)(2,1)}, bf16[1536,1024]{1,0:T(8,128)(2,1)}, u32[]{:S(2)}, u32[]{:S(2)}) collective-permute-start(bf16[1536,1024]{1,0:T(8,128)(2,1)} %rows_ref.1), channel_id=1, source_target_pairs={{0,1},{1,0},{2,3},{3,2},{4,5},{5,4},{6,7},{7,6},{8,9},{9,8},{10,11... | collective-permute-start | bytes 9437192 | tf_op jit(solution)/shard_map/ppermute | solution.py:303
  6.0 23.2 %collective-permute-start.7 = (bf16[768,1024]{1,0:T(8,128)(2,1)S(1)}, bf16[768,1024]{1,0:T(8,128)(2,1)S(1)}, u32[]{:S(2)}, u32[]{:S(2)}) collective-permute-start(bf16[768,1024]{1,0:T(8,128)(2,1)S(1)} %get-tuple-element.121), channel_id=1, source_target_pairs={{2,1},{4,3},{6,5},{8,7},{10,9},{12,11},{14,13},{18,17},{20,19},{22... | collective-permute-start | bytes 4718600 | tf_op jit(solution)/shard_map/cond/branch_3_fun/ppermute | solution.py:321
  10.3 25.1 %collective-permute-start.6 = (bf16[384,1024]{1,0:T(8,128)(2,1)S(1)}, bf16[384,1024]{1,0:T(8,128)(2,1)S(1)}, u32[]{:S(2)}, u32[]{:S(2)}) collective-permute-start(bf16[384,1024]{1,0:T(8,128)(2,1)S(1)} %slice.29), channel_id=1, source_target_pairs={{2,1},{4,3},{6,5},{8,7},{10,9},{12,11},{14,13},{18,17},{20,19},{22... | collective-permute-start | bytes 2359304 | tf_op jit(solution)/shard_map/cond/branch_3_fun/ppermute | solution.py:321
  12.8 28.2 %collective-permute-start.5 = (bf16[256,1024]{1,0:T(8,128)(2,1)S(1)}, bf16[256,1024]{1,0:T(8,128)(2,1)S(1)}, u32[]{:S(2)}, u32[]{:S(2)}) collective-permute-start(bf16[256,1024]{1,0:T(8,128)(2,1)S(1)} %slice.28), channel_id=1, source_target_pairs={{2,1},{4,3},{6,5},{8,7},{10,9},{12,11},{14,13},{18,17},{20,19},{22... | collective-permute-start | bytes 1572872 | tf_op jit(solution)/shard_map/cond/branch_3_fun/ppermute | solution.py:321
  41.6 7.8 %collective-permute-start.8 = (f32[12,128]{1,0:T(8,128)S(1)}, f32[12,128]{1,0:T(8,128)}, u32[]{:S(2)}, u32[]{:S(2)}) collective-permute-start(f32[12,128]{1,0:T(8,128)S(1)} %get-tuple-element.131), channel_id=1, source_target_pairs={{1,2},{3,4},{5,6},{7,8},{9,10},{11,12},{13,14},{17,18},{19,20},{21... | collective-permute-start | bytes 18440 | tf_op jit(solution)/shard_map/cond/branch_3_fun/ppermute | solution.py:328
  49.3 1.2 %collective-permute-start.27 = (f32[12,128]{1,0:T(8,128)S(1)}, f32[12,128]{1,0:T(8,128)S(1)}, u32[]{:S(2)}, u32[]{:S(2)}) collective-permute-start(f32[12,128]{1,0:T(8,128)S(1)} %get-tuple-element.214), channel_id=1, source_target_pairs={{0,1},{1,0},{2,3},{3,2},{4,5},{5,4},{6,7},{7,6},{8,9},{9,8},{10,11... | collective-permute-start | bytes 18440 | tf_op jit(solution)/shard_map/ppermute | solution.py:342
where the time goes:
time: 52.6 us; the launch traced here: 51.8 us
  waiting for transfers between devices  20.3 us (39%)
  Pallas kernels  20.1 us (38%)
  starting transfers between devices  7.1 us (13%)
  local copies, waits for them, and re-layouts  2.27 us (4%)
  other arithmetic  1.3 us (2%)
  between operations  0.71 us (1%)
    pallas_call x1, Pallas kernels, local_best(): pl.pallas_call(local_kernel, out_shape=(VMEM((2 * rows.shape[0], rows.sha...  15.1 us
    ppermute x3, waiting for transfers between devices, branch(): got.append(lax.ppermute(part, 'rows', route))  10.6 us
    ppermute x1, waiting for transfers between devices, branch(): return (near, far, lax.ppermute(back, 'rows', back_route))  6.47 us
    ppermute x3, starting transfers between devices, branch(): got.append(lax.ppermute(part, 'rows', route))  5.8 us
    pallas_call x1, Pallas kernels, make_plan(): pl.pallas_call(functools.partial(plan_kernel, chip_blocks), out_shape=tup...  3.32 us
    slice x2, local copies, waits for them, and re-layouts, branch(): part = embeddings[start * BLOCK:(start + piece) * BLOCK]  2.27 us
    ppermute x1, waiting for transfers between devices, on_device(): other = lax.ppermute(embeddings, 'rows', swap)  2.03 us
    pallas_call x3, Pallas kernels, cross_best(): pl.pallas_call(functools.partial(cross_kernel, start, tall, wide), out_sh...  1.67 us
  transfers between devices with their start and end apart: 6, of which 5 were waited for; matrix products, arithmetic and copies ran while one was open for 4% of the time, Pallas kernels for 38%

commit v1 on v0

--- a/solution.py
+++ b/solution.py
@@ -91,14 +91,13 @@
     for bound in SIZES[:-1]:
         branch = branch + (sent > bound).astype(jnp.int32)
     way_ref[0] = jnp.where(live, branch, 0)
-    plan_ref[0] = (live & (rightwards == upper)).astype(jnp.int32)
-    plan_ref[1] = jnp.where(receives, sent, 0)
-    plan_ref[2] = jnp.where(receives, jnp.minimum(paired, here), 0)
-    plan_ref[3] = jnp.where(receives, jnp.maximum(paired - here, 0), 0)
-    plan_ref[4] = upper
-    plan_ref[5] = me * here
-    plan_ref[6] = jnp.where(upper == 1, above, below)
-    plan_ref[7] = jnp.where(upper == 1, below, above)
+    plan_ref[0] = jnp.where(receives, sent, 0)
+    plan_ref[1] = jnp.where(receives, jnp.minimum(paired, here), 0)
+    plan_ref[2] = jnp.where(receives, jnp.maximum(paired - here, 0), 0)
+    plan_ref[3] = upper
+    plan_ref[4] = me * here
+    plan_ref[5] = jnp.where(upper == 1, above, below)
+    plan_ref[6] = jnp.where(upper == 1, below, above)
     for copy in copies:
         copy.wait()
 
@@ -107,7 +106,7 @@
     chips = block_cluster.shape[0] // chip_blocks
     return pl.pallas_call(
         functools.partial(plan_kernel, chip_blocks),
-        out_shape=tuple(jax.ShapeDtypeStruct((n,), jnp.int32) for n in (1, 8))
+        out_shape=tuple(jax.ShapeDtypeStruct((n,), jnp.int32) for n in (1, 7))
         + (VMEM((LEADING * BLOCK, rows.shape[1]), rows.dtype),) * 2,
         in_specs=[pl.BlockSpec(memory_space=SMEM), pl.BlockSpec(memory_space=pl.ANY)],
         out_specs=(pl.BlockSpec(memory_space=SMEM),) * 2 + (pl.BlockSpec(memory_space=VMEM),) * 2,
@@ -135,7 +134,7 @@
 
 def local_kernel(cluster_ref, plan_ref, rows_ref, other_ref, chip_ref, best_ref):
     blocks = rows_ref.shape[0] // BLOCK
-    upper, first, theirs = plan_ref[4], plan_ref[5], plan_ref[7]
+    upper, first, theirs = plan_ref[3], plan_ref[4], plan_ref[6]
     tall, wide = 4, 2
     size = wide * BLOCK
 
@@ -215,7 +214,8 @@
     half = 16
     rows, row_best, chip_best = refs[-3:]
     back_ref, near_best_ref, far_best_ref = refs[-6:-3]
-    count, near, far, upper = plan_ref[1], plan_ref[2], plan_ref[3], plan_ref[4]
+    whole = tall == 2
+    count, near, far, upper = plan_ref[0], plan_ref[1], plan_ref[2], plan_ref[3]
     befores = refs[: len(refs) - 6]
     for ref, before in zip((near_best_ref, far_best_ref, back_ref), befores):
         ref[...] = before[...]
@@ -236,12 +236,14 @@
         first = start + step * tall
         fits_in = [(first + i >= got_from) & (first + i < got_to) for i in range(tall)]
 
-        def tile(turn, _):
-            turn = jnp.where(turn < near_tiles, near_tile + turn, far_tile + turn - near_tiles)
-            side = chip_ref[pl.ds(pl.multiple_of(turn * wide * BLOCK, wide * BLOCK), wide * BLOCK), :]
+        def tile(turn, _, lowest, wide):
+            if whole and wide == blocks:
+                side = chip_ref[: blocks * BLOCK, :]
+            else:
+                side = chip_ref[pl.ds(pl.multiple_of(lowest * BLOCK, wide * BLOCK), wide * BLOCK), :]
             product = products(rows[...], side)
             for j in range(wide):
-                block = turn * wide + j
+                block = lowest + j
                 fits = ((block >= near_from) & (block < near_from + near)) | (
                     (block >= far_from) & (block < far_from + far)
                 )
@@ -256,7 +258,15 @@
                 chip_best[at, :] = jnp.maximum(chip_best[at, :], best)
             return 0
 
-        lax.fori_loop(0, near_tiles + far_tiles, tile, 0)
+        def one_of_both(turn, _):
+            turn = jnp.where(turn < near_tiles, near_tile + turn, far_tile + turn - near_tiles)
+            return tile(turn, 0, turn * wide, wide)
+
+        if whole:
+            tile(0, 0, 0, blocks)
+            lax.fori_loop(far_tile, far_tile + far_tiles, lambda turn, _: tile(turn, 0, turn * wide, wide), 0)
+        else:
+            lax.fori_loop(0, near_tiles + far_tiles, one_of_both, 0)
         for i in range(tall):
             top = jnp.max(row_best[i * BLOCK : (i + 1) * BLOCK, :].T, axis=0, keepdims=True)
             back_ref[pl.ds(first + i, 1), :] = jnp.where(fits_in[i], top, NEVER)
@@ -299,6 +309,7 @@
     swap = [(i, i ^ 1) for i in range(devices)]
     leftwards = [(i + 1, i) for i in range(1, devices - 1, 2)]
     rightwards = [(b, a) for a, b in leftwards]
+    upper = lax.rem(lax.axis_index("rows"), 2)
 
     other = lax.ppermute(embeddings, "rows", swap)
     way, plan, first, last = make_plan(block_cluster, embeddings, 2 * blocks)
@@ -322,26 +333,23 @@
             chip, best = local_best(block_cluster, plan, embeddings, other)
             found = (best,)
             for start, piece in zip(starts, got):
-                wide = 4 if start == starts[-1] else 2
+                wide = 2
                 back, near, far = cross_best(plan, start, piece, chip, found, wide)
                 found = near, far, back
-            return near, far, lax.ppermute(back, "rows", back_route)
+            returned = lax.ppermute(back, "rows", back_route)
+            sender = upper == (0 if to_left else 1)
+            return jnp.maximum(near, jnp.where(sender, returned, NEVER)), far
 
         return branch
 
     def stay(embeddings, first, last, other):
         _, best = local_best(block_cluster, plan, embeddings, other)
-        nothing = jnp.full((blocks, BLOCK), NEVER, jnp.float32)
-        return best, nothing, nothing
+        return best, jnp.full((blocks, BLOCK), NEVER, jnp.float32)
 
     sends = [send(leftwards, rightwards, pieces) for pieces in PIECES]
     sends += [send(rightwards, leftwards, pieces) for pieces in PIECES]
-    best, far_best, returned = lax.switch(
-        way[0], [stay] + sends, embeddings, first, last, other
-    )
-    best = jnp.maximum(best, lax.ppermute(far_best, "rows", swap))
-    best = jnp.where(plan[0] > 0, jnp.maximum(best, returned), best)
-    return best.reshape(-1)
+    best, far_best = lax.switch(way[0], [stay] + sends, embeddings, first, last, other)
+    return jnp.maximum(best, lax.ppermute(far_best, "rows", swap)).reshape(-1)
 
 
 def solution(mesh):

time: 52.6 us -> 50.1 us (0.952)
  the two profiles are of different devices: /device:TPU:8 before, /device:TPU:7 now
where the time goes in v1:
time: 50.1 us; the launch traced here: 49.1 us
  starting transfers between devices  22.7 us (45%)
  Pallas kernels  13.1 us (26%)
  waiting for transfers between devices  9.56 us (19%)
  local copies, waits for them, and re-layouts  2.43 us (5%)
  between operations  0.67 us (1%)
  other arithmetic  0.61 us (1%)
    ppermute x1, starting transfers between devices, on_device(): return jnp.maximum(best, lax.ppermute(far_best, 'rows', swap)).reshape(-1)  11.2 us
    ppermute x1, starting transfers between devices, branch(): returned = lax.ppermute(back, 'rows', back_route)  9.49 us
    pallas_call x1, Pallas kernels, local_best(): pl.pallas_call(local_kernel, out_shape=(VMEM((2 * rows.shape[0], rows.sha...  8.39 us
    ppermute x1, waiting for transfers between devices, branch(): got.append(lax.ppermute(part, 'rows', route))  7.32 us
    pallas_call x1, Pallas kernels, make_plan(): pl.pallas_call(functools.partial(plan_kernel, chip_blocks), out_shape=tup...  3.18 us
    pallas_call x1, Pallas kernels, cross_best(): pl.pallas_call(functools.partial(cross_kernel, start, tall, wide), out_sh...  1.52 us
    slice x1, local copies, waits for them, and re-layouts, branch(): part = embeddings[start * BLOCK:(start + piece) * BLOCK]  1.29 us
    ppermute x1, starting transfers between devices, branch(): got.append(lax.ppermute(part, 'rows', route))  1.29 us
  transfers between devices with their start and end apart: 4, of which 4 were waited for; matrix products, arithmetic and copies ran while one was open for 0% of the time, Pallas kernels for 24%

profile of v1, /device:TPU:7, one launch (start us, length us, event | category | flops | bytes accessed | tf_op | source)
XLA Modules:
  0.0 49.1 jit_solution(15292987873453234189)
XLA Ops:
  0.0 0.0 copy-start.3
  0.0 0.7 %collective-permute-start.26 = (bf16[1536,1024]{1,0:T(8,128)(2,1)}, bf16[1536,1024]{1,0:T(8,128)(2,1)}, u32[]{:S(2)}, u32[]{:S(2)}) collective-permute-start(bf16[1536,1024]{1,0:T(8,128)(2,1)} %rows_ref.1), channel_id=1, source_target_pairs={{0,1},{1,0},{2,3},{3,2},{4,5},{5,4},{6,7},{7,6},{8,9},{9,8},{10,11... | collective-permute-start | bytes 9437192 | tf_op jit(solution)/shard_map/ppermute | solution.py:314
  0.7 3.2 %shard_map.28 = (s32[1]{0:T(128)}, s32[7]{0:T(128)S(1)}, bf16[768,1024]{1,0:T(8,128)(2,1)S(1)}, bf16[768,1024]{1,0:T(8,128)(2,1)S(1)}) custom-call(s32[192]{0:T(256)} %cluster_ref.1, bf16[1536,1024]{1,0:T(8,128)(2,1)} %rows_ref.1), custom_call_target="tpu_custom_call" | custom-call | tf_op jit(solution)/shard_map/pallas_call | solution.py:107
  3.9 0.0 copy-start
  3.9 1.1 %copy-done = bf16[768,1024]{1,0:T(8,128)(2,1)} copy-done((bf16[768,1024]{1,0:T(8,128)(2,1)}, bf16[768,1024]{1,0:T(8,128)(2,1)S(1)}, u32[]{:S(2)}) %copy-start) | copy-done | bytes 1572888
  5.7 0.6 %collective-permute-done.26 = bf16[1536,1024]{1,0:T(8,128)(2,1)} collective-permute-done((bf16[1536,1024]{1,0:T(8,128)(2,1)}, bf16[1536,1024]{1,0:T(8,128)(2,1)}, u32[]{:S(2)}, u32[]{:S(2)}) %collective-permute-start.26) | collective-permute-done | bytes 3145760 | tf_op jit(solution)/shard_map/ppermute | solution.py:314
  6.3 0.0 copy-done.3
  6.3 30.1 %conditional.1 = (f32[12,128]{1,0:T(8,128)S(1)}, f32[12,128]{1,0:T(8,128)S(1)}) conditional(s32[]{:T(128)} %bitcast, (s32[192]{0:T(256)S(1)}, s32[7]{0:T(128)S(1)}, bf16[1536,1024]{1,0:T(8,128)(2,1)}, bf16[1536,1024]{1,0:T(8,128)(2,1)}) %tuple.57, (bf16[1536,1024]{1,0:T(8,128)(2,1)}, s32[192]{0:T(256)S(1)}, ...), branch_computations={%region_0.0_spmd, %region_1.2_spmd, %region_2.3_spmd, %region_3.4_... | conditional | flops 14495517696 | bytes 47229140 | solution.py:351
  6.3 1.3 %slice.24 = bf16[512,1024]{1,0:T(8,128)(2,1)S(1)} slice(bf16[1536,1024]{1,0:T(8,128)(2,1)} %get-tuple-element.111.rows_ref), slice={[0:512], [0:1024]} | slice | bytes 2097152 | tf_op jit(solution)/shard_map/cond/branch_1_fun/slice | solution.py:331
  7.6 1.3 %collective-permute-start = (bf16[512,1024]{1,0:T(8,128)(2,1)S(1)}, bf16[512,1024]{1,0:T(8,128)(2,1)S(1)}, u32[]{:S(2)}, u32[]{:S(2)}) collective-permute-start(bf16[512,1024]{1,0:T(8,128)(2,1)S(1)} %slice.24), channel_id=1, source_target_pairs={{2,1},{4,3},{6,5},{8,7},{10,9},{12,11},{14,13},{18,17},{20,19},{22... | collective-permute-start | bytes 3145736 | tf_op jit(solution)/shard_map/cond/branch_1_fun/ppermute | solution.py:332
  8.9 8.4 %branch_1_fun.2 = (bf16[3072,1024]{1,0:T(8,128)(2,1)S(1)}, f32[12,128]{1,0:T(8,128)S(1)}) custom-call(s32[192]{0:T(256)S(1)} %get-tuple-element.112.cluster_ref, s32[7]{0:T(128)S(1)} %get-tuple-element.110.plan_ref, bf16[1536,1024]{1,0:T(8,128)(2,1)} %get-tuple-element.111.rows_ref, bf16[1536,1024]{1,0:T(8,128)(2,1)} %get-tuple-element.113.other_ref), custom_call_target="tpu_custom_call" | custom-call | flops 9663676416 | bytes 12582912 | tf_op jit(solution)/shard_map/cond/branch_1_fun/pallas_call | solution.py:199
  17.3 7.3 %collective-permute-done.got_ref = bf16[512,1024]{1,0:T(8,128)(2,1)S(1)} collective-permute-done((bf16[512,1024]{1,0:T(8,128)(2,1)S(1)}, bf16[512,1024]{1,0:T(8,128)(2,1)S(1)}, u32[]{:S(2)}, u32[]{:S(2)}) %collective-permute-start) | collective-permute-done | bytes 1048608 | tf_op jit(solution)/shard_map/cond/branch_1_fun/ppermute | solution.py:332
  24.6 1.5 %branch_1_fun.3 = (f32[12,128]{1,0:T(8,128)S(1)}, f32[12,128]{1,0:T(8,128)S(1)}, f32[12,128]{1,0:T(8,128)S(1)}) custom-call(s32[7]{0:T(128)S(1)} %get-tuple-element.110.plan_ref, bf16[512,1024]{1,0:T(8,128)(2,1)S(1)} %collective-permute-done.got_ref, bf16[3072,1024]{1,0:T(8,128)(2,1)S(1)} %get-tuple-element.114.chip_ref, ...), custom_call_target="tpu_custom_call" | custom-call | flops 1610612736 | bytes 2097152 | tf_op jit(solution)/shard_map/cond/branch_1_fun/pallas_call | solution.py:291
  26.2 9.5 %collective-permute-start.1 = (f32[12,128]{1,0:T(8,128)S(1)}, f32[12,128]{1,0:T(8,128)S(1)}, u32[]{:S(2)}, u32[]{:S(2)}) collective-permute-start(f32[12,128]{1,0:T(8,128)S(1)} %get-tuple-element.118), channel_id=1, source_target_pairs={{1,2},{3,4},{5,6},{7,8},{9,10},{11,12},{13,14},{17,18},{19,20},{21... | collective-permute-start | bytes 18440 | tf_op jit(solution)/shard_map/cond/branch_1_fun/ppermute | solution.py:339
  35.7 0.8 %collective-permute-done.1 = f32[12,128]{1,0:T(8,128)S(1)} collective-permute-done((f32[12,128]{1,0:T(8,128)S(1)}, f32[12,128]{1,0:T(8,128)S(1)}, u32[]{:S(2)}, u32[]{:S(2)}) %collective-permute-start.1) | collective-permute-done | bytes 6176 | tf_op jit(solution)/shard_map/cond/branch_1_fun/ppermute | solution.py:339
  36.4 11.2 %collective-permute-start.27 = (f32[12,128]{1,0:T(8,128)S(1)}, f32[12,128]{1,0:T(8,128)S(1)}, u32[]{:S(2)}, u32[]{:S(2)}) collective-permute-start(f32[12,128]{1,0:T(8,128)S(1)} %get-tuple-element.237), channel_id=1, source_target_pairs={{0,1},{1,0},{2,3},{3,2},{4,5},{5,4},{6,7},{7,6},{8,9},{9,8},{10,11... | collective-permute-start | bytes 18440 | tf_op jit(solution)/shard_map/ppermute | solution.py:352
  47.7 0.8 %collective-permute-done.27 = f32[12,128]{1,0:T(8,128)S(1)} collective-permute-done((f32[12,128]{1,0:T(8,128)S(1)}, f32[12,128]{1,0:T(8,128)S(1)}, u32[]{:S(2)}, u32[]{:S(2)}) %collective-permute-start.27) | collective-permute-done | bytes 6176 | tf_op jit(solution)/shard_map/ppermute | solution.py:352
  48.5 0.6 %maximum_bitcast_fusion = f32[1536]{0:T(1024)} fusion(f32[12,128]{1,0:T(8,128)S(1)} %get-tuple-element.236, f32[12,128]{1,0:T(8,128)S(1)} %collective-permute-done.27), kind=kLoop, calls=%fused_computation.8 | loop fusion | flops 1536 | bytes 18432 | tf_op jit(solution)/shard_map/reshape | solution.py:352
  (1 shorter events, 0.0 us)
Async XLA Ops:
  0.0 6.3 %copy-start.3 = (s32[192]{0:T(256)S(1)}, s32[192]{0:T(256)}, u32[]{:S(2)}) copy-start(s32[192]{0:T(256)} %cluster_ref.1) | copy-start | bytes 2308
  0.0 6.3 %collective-permute-start.26 = (bf16[1536,1024]{1,0:T(8,128)(2,1)}, bf16[1536,1024]{1,0:T(8,128)(2,1)}, u32[]{:S(2)}, u32[]{:S(2)}) collective-permute-start(bf16[1536,1024]{1,0:T(8,128)(2,1)} %rows_ref.1), channel_id=1, source_target_pairs={{0,1},{1,0},{2,3},{3,2},{4,5},{5,4},{6,7},{7,6},{8,9},{9,8},{10,11... | collective-permute-start | bytes 9437192 | tf_op jit(solution)/shard_map/ppermute | solution.py:314
  3.9 1.1 %copy-start = (bf16[768,1024]{1,0:T(8,128)(2,1)}, bf16[768,1024]{1,0:T(8,128)(2,1)S(1)}, u32[]{:S(2)}) copy-start(bf16[768,1024]{1,0:T(8,128)(2,1)S(1)} %get-tuple-element.234) | copy-start | bytes 4718596
  7.6 17.0 %collective-permute-start = (bf16[512,1024]{1,0:T(8,128)(2,1)S(1)}, bf16[512,1024]{1,0:T(8,128)(2,1)S(1)}, u32[]{:S(2)}, u32[]{:S(2)}) collective-permute-start(bf16[512,1024]{1,0:T(8,128)(2,1)S(1)} %slice.24), channel_id=1, source_target_pairs={{2,1},{4,3},{6,5},{8,7},{10,9},{12,11},{14,13},{18,17},{20,19},{22... | collective-permute-start | bytes 3145736 | tf_op jit(solution)/shard_map/cond/branch_1_fun/ppermute | solution.py:332
  26.2 10.3 %collective-permute-start.1 = (f32[12,128]{1,0:T(8,128)S(1)}, f32[12,128]{1,0:T(8,128)S(1)}, u32[]{:S(2)}, u32[]{:S(2)}) collective-permute-start(f32[12,128]{1,0:T(8,128)S(1)} %get-tuple-element.118), channel_id=1, source_target_pairs={{1,2},{3,4},{5,6},{7,8},{9,10},{11,12},{13,14},{17,18},{19,20},{21... | collective-permute-start | bytes 18440 | tf_op jit(solution)/shard_map/cond/branch_1_fun/ppermute | solution.py:339
  36.4 12.1 %collective-permute-start.27 = (f32[12,128]{1,0:T(8,128)S(1)}, f32[12,128]{1,0:T(8,128)S(1)}, u32[]{:S(2)}, u32[]{:S(2)}) collective-permute-start(f32[12,128]{1,0:T(8,128)S(1)} %get-tuple-element.237), channel_id=1, source_target_pairs={{0,1},{1,0},{2,3},{3,2},{4,5},{5,4},{6,7},{7,6},{8,9},{9,8},{10,11... | collective-permute-start | bytes 18440 | tf_op jit(solution)/shard_map/ppermute | solution.py:352
